TPU v7x, 32 devices: a whole 2x2x4 slice. The times are simulated.
32 devices in a mesh: dp: 8 (over y, x, core), tensor: 4 (over z).
Axes of the slice: x: 2, y: 2, z: 4, core: 2. Of those that a mesh axis runs over, the one named last changes fastest.
Arguments:
- tokens: bfloat16 [16384, 768], P(('dp', 'tensor')), may hold values from -6 to 6
- cotangent: bfloat16 [16384, 768], P(('dp', 'tensor')), may hold values from -6 to 6, as said below
- segment: int32 [32, 512], P(('dp', 'tensor')), may hold values from 0 to 11, never falling along the last dimension, each value on 1 to 202 neighbouring positions
- projection: float32 [64, 32], replicated, may hold values from -5 to 5
- first_gain: float32 [768], replicated, may hold values from 0.5 to 1.5
- first_bias: float32 [768], replicated, may hold values from -4 to 4
- w_query: bfloat16 [768, 768], replicated, may hold values from -0.109375 to 0.109375
- w_key: bfloat16 [768, 768], replicated, may hold values from -0.109375 to 0.109375
- w_value: bfloat16 [768, 768], replicated, may hold values from -0.21875 to 0.21875
- w_out: bfloat16 [768, 768], replicated, may hold values from -1.25 to 1.25
- b_query: float32 [768], replicated, may hold values from -4 to 4
- b_key: float32 [768], replicated, may hold values from -4 to 4
- b_value: float32 [768], replicated, may hold values from -4 to 4
- b_out: float32 [768], replicated, may hold values from -4 to 4
- second_gain: float32 [768], replicated, may hold values from 0.5 to 1.5
- second_bias: float32 [768], replicated, may hold values from -4 to 4
- w_up: bfloat16 [768, 3072], P(None, 'tensor'), may hold values from -0.21875 to 0.21875
- b_up: float32 [3072], P('tensor'), may hold values from -4 to 4
- w_down: bfloat16 [3072, 768], P('tensor'), may hold values from -0.109375 to 0.109375
- b_down: float32 [768], replicated, may hold values from -4 to 4
Outputs:
- output: bfloat16 [16384, 768], P(('dp', 'tensor'))
- grad_tokens: bfloat16 [16384, 768], P(('dp', 'tensor'))
- grad_first_gain: float32 [768], replicated
- grad_first_bias: float32 [768], replicated
- grad_w_query: float32 [768, 768], replicated
- grad_w_key: float32 [768, 768], replicated
- grad_w_value: float32 [768, 768], replicated
- grad_w_out: float32 [768, 768], replicated
- grad_b_query: float32 [768], replicated
- grad_b_key: float32 [768], replicated
- grad_b_value: float32 [768], replicated
- grad_b_out: float32 [768], replicated
- grad_second_gain: float32 [768], replicated
- grad_second_bias: float32 [768], replicated
- grad_w_up: float32 [768, 3072], P(None, 'tensor')
- grad_b_up: float32 [3072], P('tensor')
- grad_w_down: float32 [3072, 768], P('tensor')
- grad_b_down: float32 [768], replicated
Inputs may be any that keep to these rules, and one draw needn't show every extreme that they name: `segment`: within each row of 512 tokens, molecule numbers never fall; each molecule has 1 to 202 tokens and one has exactly 202. `cotangent`: gradient rows of order one.
All inputs are finite; a program needn't handle non-finite values.
Results may differ from a plain program's by a relative error of at most 0.01.
Values may be sent and summed in bfloat16 or wider, within the bound.
No kernel may reach another device: no remote copies, remote signals or barrier semaphores. Data moves between devices by JAX's collectives and lax.ppermute only.
A program may use at most 192 MiB of HBM per device.

v0:
```python
from functools import partial
import math
import jax
import jax.numpy as jnp
from jax import lax
from jax.sharding import PartitionSpec as P

HEADS = 12
highest_precision = lax.Precision.HIGHEST


def layer_norm(inputs, gain, shift):
    average = jnp.mean(inputs, -1, keepdims=True)
    centred = inputs - average
    spread = jnp.mean(centred * centred, -1, keepdims=True)
    return centred * lax.rsqrt(spread + 1e-05) * gain + shift


def positions(labels):
    places = jnp.arange(labels.shape[0], dtype=jnp.int32)
    matches = labels[:, None] == labels[None, :]
    before = places[None, :] < places[:, None]
    return jnp.sum((matches & before).astype(jnp.int32), axis=1)


def rotate(inputs, places):
    split_at = inputs.shape[-1] // 2
    ladder = jnp.arange(split_at).astype(jnp.float32)
    speeds = jnp.exp(ladder * (-2.0 * math.log(10000.0) / inputs.shape[-1]))
    angles = places.astype(jnp.float32)[:, None] * speeds[None, :]
    cosine = jnp.cos(angles)[:, None, :]
    sine_part = jnp.sin(angles)[:, None, :]
    lower_half = inputs[..., :split_at]
    upper_half = inputs[..., split_at:]
    return jnp.concatenate(
        [
            lower_half * cosine - upper_half * sine_part,
            upper_half * cosine + lower_half * sine_part,
        ],
        -1,
    )


def features(inputs, projection):
    scaled = inputs * inputs.shape[-1] ** (-0.25)
    projected = jnp.einsum("rhd,df->rhf", scaled, projection, precision=highest_precision)
    return jnp.exp(
        projected - 0.5 * jnp.sum(scaled * scaled, -1, keepdims=True)
    ) * projection.shape[-1] ** (-0.5)


def attend(queries, key_rows, value_rows, labels, projection):
    row_count = queries.shape[0]
    places = positions(labels)
    query_feature_map = features(rotate(queries.reshape(row_count, HEADS, -1), places), projection)
    key_feature_map = features(rotate(key_rows.reshape(row_count, HEADS, -1), places), projection)
    value_heads = value_rows.reshape(row_count, HEADS, -1)
    attention_scores = jnp.einsum(
        "otg,atg->toa", query_feature_map, key_feature_map, precision=highest_precision
    )
    matches = (labels[:, None] == labels[None, :]).astype(attention_scores.dtype)
    weights = attention_scores * matches[None]
    totals = jnp.sum(weights, -1)
    mixture = jnp.einsum("hqk,khd->qhd", weights, value_heads, precision=highest_precision)
    return (mixture / jnp.transpose(totals)[:, :, None]).reshape(row_count, -1)


def matmul(left, right):
    return jnp.dot(left, right, preferred_element_type=jnp.float32)


def left_product(left, right):
    return lax.dot_general(
        left, right, (((0,), (0,)), ((), ())), preferred_element_type=jnp.float32
    )


def right_product(left, right):
    return lax.dot_general(
        left, right, (((1,), (1,)), ((), ())), preferred_element_type=jnp.float32
    )


def column_sum(values):
    return jnp.sum(values.astype(jnp.float32), 0)


def body(
    tokens,
    cotangent,
    segment,
    projection,
    first_gain,
    first_bias,
    w_query,
    w_key,
    w_value,
    w_out,
    b_query,
    b_key,
    b_value,
    b_out,
    second_gain,
    second_bias,
    w_up,
    b_up,
    w_down,
    b_down,
):
    row_count = tokens.shape[0]
    labels = segment[0]
    widened = tokens.astype(jnp.float32)
    normed, first_back = jax.vjp(layer_norm, widened, first_gain, first_bias)
    normed_low = normed.astype(jnp.bfloat16)
    queries = matmul(normed_low, w_query) + b_query
    key_rows = matmul(normed_low, w_key) + b_key
    value_rows = matmul(normed_low, w_value) + b_value

    def attend_here(query_in, key_in, value_in):
        return attend(query_in, key_in, value_in, labels, projection)

    context, kernel_core_pullback = jax.vjp(attend_here, queries, key_rows, value_rows)
    context_low = context.astype(jnp.bfloat16)
    middle = widened + matmul(context_low, w_out) + b_out
    second, second_back = jax.vjp(layer_norm, middle, second_gain, second_bias)
    second_low = second.astype(jnp.bfloat16)
    upstream = cotangent.astype(jnp.float32)
    down_bias_grad = jnp.sum(upstream, 0)
    gathered = lax.all_gather(second_low, "tensor", axis=0, tiled=True)
    inner_rows = matmul(gathered, w_up) + b_up
    hidden, gelu_back = jax.vjp(partial(jax.nn.gelu, approximate=False), inner_rows)
    hidden_low = hidden.astype(jnp.bfloat16)
    branch = lax.psum_scatter(
        matmul(
            lax.slice_in_dim(hidden_low, 0, row_count * lax.axis_size("tensor"), axis=0), w_down
        ).astype(jnp.bfloat16),
        "tensor",
        scatter_dimension=0,
        tiled=True,
    ).astype(jnp.float32)
    output = (middle + branch + b_down).astype(jnp.bfloat16)
    cot_gathered = lax.all_gather(cotangent, "tensor", axis=0, tiled=True)
    down_grad = left_product(hidden_low, cot_gathered)
    hidden_grad = right_product(cot_gathered, w_down)
    inner_grad = gelu_back(hidden_grad)[0].astype(jnp.bfloat16)
    up_bias_grad = column_sum(inner_grad)
    up_grad = left_product(gathered, inner_grad)
    second_grad = lax.psum_scatter(
        right_product(inner_grad, w_up).astype(jnp.bfloat16),
        "tensor",
        scatter_dimension=0,
        tiled=True,
    ).astype(jnp.float32)
    up_grad, up_bias_grad, down_grad = lax.psum((up_grad, up_bias_grad, down_grad), "dp")
    middle_back, gain_two_grad, bias_two_grad = second_back(second_grad)
    middle_grad = upstream + middle_back
    out_grad_low = middle_grad.astype(jnp.bfloat16)
    wout_grad = left_product(context_low, out_grad_low)
    bout_grad = column_sum(out_grad_low)
    context_grad = right_product(out_grad_low, w_out)
    query_grad, key_grad, value_grad = kernel_core_pullback(context_grad)
    query_low = query_grad.astype(jnp.bfloat16)
    key_low = key_grad.astype(jnp.bfloat16)
    value_low = value_grad.astype(jnp.bfloat16)
    query_weight_grad = left_product(normed_low, query_low)
    wkey_grad = left_product(normed_low, key_low)
    value_weight_grad = left_product(normed_low, value_low)
    bquery_grad = column_sum(query_low)
    bkey_grad = column_sum(key_low)
    bvalue_grad = column_sum(value_low)
    normed_grad = (
        right_product(query_low, w_query)
        + right_product(key_low, w_key)
        + right_product(value_low, w_value)
    )
    token_back, gain_one_grad, bias_one_grad = first_back(normed_grad)
    grad_tokens = (middle_grad + token_back).astype(jnp.bfloat16)
    (
        gain_one_grad,
        bias_one_grad,
        query_weight_grad,
        wkey_grad,
        value_weight_grad,
        wout_grad,
        bquery_grad,
        bkey_grad,
        bvalue_grad,
        bout_grad,
        gain_two_grad,
        bias_two_grad,
        down_bias_grad,
    ) = lax.psum(
        (
            gain_one_grad,
            bias_one_grad,
            query_weight_grad,
            wkey_grad,
            value_weight_grad,
            wout_grad,
            bquery_grad,
            bkey_grad,
            bvalue_grad,
            bout_grad,
            gain_two_grad,
            bias_two_grad,
            down_bias_grad,
        ),
        ("dp", "tensor"),
    )
    return (
        output,
        grad_tokens,
        gain_one_grad,
        bias_one_grad,
        query_weight_grad,
        wkey_grad,
        value_weight_grad,
        wout_grad,
        bquery_grad,
        bkey_grad,
        bvalue_grad,
        bout_grad,
        gain_two_grad,
        bias_two_grad,
        up_grad,
        up_bias_grad,
        down_grad,
        down_bias_grad,
    )


def solution(mesh):
    return jax.shard_map(
        body,
        mesh=mesh,
        in_specs=(
            P(("dp", "tensor"), None),
            P(("dp", "tensor"), None),
            P(("dp", "tensor"), None),
            P(),
            P(),
            P(),
            P(),
            P(),
            P(),
            P(),
            P(),
            P(),
            P(),
            P(),
            P(),
            P(),
            P(None, "tensor"),
            P("tensor"),
            P("tensor", None),
            P(),
        ),
        out_specs=(
            P(("dp", "tensor"), None),
            P(("dp", "tensor"), None),
            P(),
            P(),
            P(),
            P(),
            P(),
            P(),
            P(),
            P(),
            P(),
            P(),
            P(),
            P(),
            P(None, "tensor"),
            P("tensor"),
            P("tensor", None),
            P(),
        ),
        check_vma=False,
    )
```

profile of v0, /device:TPU:0, one launch (start us, length us, event | category | flops | bytes accessed | tf_op | source)
XLA Modules:
  0.0 651.4 jit_solution(13527128081990880448)
XLA Ops:
  9.8 2.1 convolution_add_fusion.1
  11.9 3.0 copy.50
  14.9 3.3 convolution_add_fusion
  18.3 3.0 copy.51
  21.6 2.3 multiply_subtract_fusion.1
  25.1 2.0 fusion.53
  27.1 2.0 fusion.59
  29.0 2.1 convolution_add_fusion.2
  31.1 3.0 copy.49
  34.1 12.6 %multiply_reduce_fusion = (f32[12,512]{1,0:T(8,128)S(1)}, f32[12,512,512]{1,2,0:T(8,128)S(1)}) fusion(f32[512,512]{0,1:T(8,128)S(1)} %compare_convert_fusion, f32[512,12,32]{0,2,1:T(8,128)} %fusion.59, f32[512,12,32]{0,2,1:T(8,128)} %fusion.53), kind=kOutput, calls=%fused_computation.5 | convolution fusion | flops 1214638080 | bytes 15228928 | tf_op jit(solution)/shard_map/jvp(otg,atg->toa)/dot_general | solution.py:58
  46.7 9.7 %fusion.37 = (bf16[512,12,64]{0,2,1:T(8,128)(2,1)S(1)}, f32[12,64,512]{2,1,0:T(8,128)}) fusion(f32[512,12]{0,1:T(8,128)S(1)} %bitcast.95, f32[512,12,64]{0,2,1:T(8,128)S(1)} %bitcast.84, f32[12,512,512]{1,2,0:T(8,128)S(1)} %get-tuple-element.69, f32[512,512]{0,1:T(8,128)S(1)} %compare_convert_fusion), kind=kOutput, calls=%fused_computation.67 | convolution fusion | flops 2419851264 | bytes 17588224 | tf_op jit(solution)/shard_map/jvp(hqk,khd->qhd)/dot_general | solution.py:64
  60.5 65.5 %all-gather.3.cloned.1.call-done = bf16[2048,768]{1,0:T(8,128)(2,1)} async-done(((bf16[512,768]{1,0:T(8,128)(2,1)}), bf16[2048,768]{1,0:T(8,128)(2,1)}) %all-gather.3.cloned.1.call-update) | async-done | bytes 3145744 | tf_op jit(solution)/shard_map/all_gather | solution.py:129
  126.1 7.4 %fusion.109 = f32[2048,768]{1,0:T(8,128)} fusion(bf16[2048,768]{1,0:T(8,128)(2,1)} %all-gather.3.cloned.1.call-done, bf16[768,768]{1,0:T(8,128)(2,1)} %param.36), kind=kOutput, calls=%fused_computation.167 | convolution fusion | flops 2415919104 | bytes 10616832 | tf_op jit(solution)/shard_map/dot_general | solution.py:69
  133.5 56.3 %all-gather.5.cloned.1.call-done = bf16[2048,768]{1,0:T(8,128)(2,1)} async-done(((bf16[512,768]{1,0:T(8,128)(2,1)}), bf16[2048,768]{1,0:T(8,128)(2,1)}) %all-gather.5.cloned.1.call-update) | async-done | bytes 3145744 | tf_op jit(solution)/shard_map/all_gather | solution.py:142
  189.8 19.6 %convert_reduce_fusion = (f32[768]{0:T(1024)S(1)}, bf16[2048,768]{1,0:T(8,128)(2,1)S(1)}, f32[2048,768]{1,0:T(8,128)}) fusion(f32[2048,768]{1,0:T(8,128)} %fusion.109, f32[768]{0:T(1024)S(1)} %copy-done.41, bf16[2048,768]{1,0:T(8,128)(2,1)} %all-gather.5.cloned.1.call-done, bf16[768,768]{1,0:T(8,128)(2,1)S(1)} %copy-done), kind=kOutput, calls=%fused_computation.10 | convolution fusion | flops 2533883136 | bytes 20060160 | tf_op jit(solution)/shard_map/dot_general | solution.py:79
  209.4 1.7 copy-done.54
  211.2 4.0 convolution_convert_fusion
  215.3 5.5 multiply_convert_fusion
  220.8 1.6 copy-done.24
  222.4 3.9 convolution_convert_fusion.1
  226.5 7.1 %fusion.114 = f32[768,768]{1,0:T(8,128)} fusion(bf16[2048,768]{1,0:T(8,128)(2,1)} %all-gather.3.cloned.1.call-done, bf16[2048,768]{1,0:T(8,128)(2,1)} %copy-done.54), kind=kOutput, calls=%fused_computation.172 | convolution fusion | flops 2415919104 | bytes 8650752 | tf_op jit(solution)/shard_map/dot_general | solution.py:73
  233.6 4.2 fusion.115
  238.3 36.0 %reduce-scatter.5.cloned.1.call-done = bf16[512,768]{1,0:T(8,128)(2,1)} async-done(((bf16[2048,768]{1,0:T(8,128)(2,1)}), bf16[512,768]{1,0:T(8,128)(2,1)}) %reduce-scatter.5.cloned.1.call-update) | async-done | bytes 786448 | tf_op jit(solution)/shard_map/reduce_scatter | solution.py:148
  274.3 2.3 fusion.33
  276.6 60.1 %reduce-scatter.3.cloned.1.call-done = bf16[512,768]{1,0:T(8,128)(2,1)} async-done(((bf16[2048,768]{1,0:T(8,128)(2,1)}), bf16[512,768]{1,0:T(8,128)(2,1)}) %reduce-scatter.3.cloned.1.call-update) | async-done | bytes 786448 | tf_op jit(solution)/shard_map/reduce_scatter | solution.py:133
  336.7 3.5 fusion.105
  343.5 10.5 %fusion.35 = f32[12,512,512]{1,2,0:T(8,128)S(1)} fusion(f32[512,12,64]{0,2,1:T(8,128)S(1)} %bitcast.85, f32[512,12,64]{0,2,1:T(8,128)S(1)} %bitcast.86, f32[512,12]{0,1:T(8,128)S(1)} %bitcast.96), kind=kOutput, calls=%fused_computation.63 | convolution fusion | flops 2416312320 | bytes 15753216 | tf_op jit(solution)/shard_map/transpose(jvp(hqk,khd->qhd))/dot_general | solution.py:64
  355.4 8.6 %fusion.108 = (f32[512,12]{0,1:T(8,128)S(1)}, f32[512,12,32]{0,2,1:T(8,128)S(1)}) fusion(f32[512,12,32]{0,2,1:T(8,128)S(1)} %copy-done.9, f32[512,12,32]{0,2,1:T(8,128)S(1)} %copy-done.10, f32[12,512,512]{1,2,0:T(8,128)S(1)} %fusion.35, f32[12,512]{1,0:T(8,128)S(1)} %negate_bitcast_fusion, f32[512,512]{0,1:T(8,128)S(1)} %compare_convert_fusion), kind=kOutput, calls=%fused_computation.166 | convolution fusion | flops 1215031296 | bytes 16039936 | tf_op jit(solution)/shard_map/transpose(jvp(otg,atg->toa))/dot_general | solution.py:58
  364.1 12.9 %fusion.107 = (f32[512,12]{0,1:T(8,128)S(1)}, f32[512,12,32]{0,2,1:T(8,128)S(1)}) fusion(f32[512,12,32]{0,2,1:T(8,128)S(1)} %copy-done.10, f32[512,12,32]{0,2,1:T(8,128)S(1)} %copy-done.9, f32[12,512,512]{1,2,0:T(8,128)S(1)} %fusion.35, f32[12,512]{1,0:T(8,128)S(1)} %negate_bitcast_fusion, f32[512,512]{0,1:T(8,128)S(1)} %compare_convert_fusion), kind=kOutput, calls=%fused_computation.165 | convolution fusion | flops 1215031296 | bytes 16039936 | tf_op jit(solution)/shard_map/transpose(jvp(otg,atg->toa))/dot_general | solution.py:58
  377.1 1.7 fusion.40
  378.8 1.7 fusion.39
  381.6 1.3 copy-done.23
  383.0 2.2 fusion.113
  385.2 2.9 fusion.95
  388.1 2.5 fusion.97
  390.6 12.1 %convert_reduce_fusion.5 = (f32[12,64]{1,0:T(8,128)S(1)}, bf16[12,64,512]{2,1,0:T(8,128)(2,1)S(1)}) fusion(f32[12,512,512]{1,2,0:T(8,128)S(1)} %bitcast.83, f32[512,512]{0,1:T(8,128)S(1)} %compare_convert_fusion, f32[512,12,64]{0,2,1:T(8,128)S(1)} %bitcast.88, f32[512,12]{0,1:T(8,128)S(1)} %bitcast.97), kind=kOutput, calls=%fused_computation.74 | convolution fusion | flops 2420636928 | bytes 16018432 | tf_op jit(solution)/shard_map/transpose(jvp(hqk,khd->qhd))/dot_general | solution.py:64
  402.7 2.5 fusion.93
  405.2 14.8 %psum.125 = f32[768]{0:T(1024)} all-reduce(f32[768]{0:T(1024)S(1)} %get-tuple-element.40), channel_id=1, replica_groups=mesh['dp'=8,'tensor'=4] {'dp'}, use_global_device_ids=true, to_apply=%region_39.0 | all-reduce | flops 768 | bytes 6144 | tf_op jit(solution)/shard_map/psum | solution.py:154
  420.2 2.3 fusion.112
  426.6 1.7 convert_reduce_fusion.3
  428.3 42.2 %all-reduce.4 = (f32[768]{0:T(1024)}, f32[768]{0:T(1024)}, f32[768]{0:T(1024)}, f32[768]{0:T(1024)}, f32[768]{0:T(1024)}, /*index=5*/f32[768]{0:T(1024)}, f32[768]{0:T(1024)}, f32[768]{0:T(1024)}, f32[768]{0:T(1024)}) all-reduce(f32[768]{0:T(1024)S(1)} %get-tuple-element.18, ...), channel_id=1, replica_groups=mesh['dp'=8,'tensor'=4] {'dp','tensor'}, use_global_device_ids=true, to_apply=%region_18.0 | all-reduce | flops 6912 | bytes 55296 | tf_op jit(solution)/shard_map/psum | solution.py:192
  470.5 159.0 %all-reduce.10.cloned.1.call-done = (f32[768,768]{1,0:T(8,128)}, f32[768,768]{1,0:T(8,128)}, f32[768,768]{1,0:T(8,128)}, f32[768,768]{1,0:T(8,128)}) async-done(((f32[768,768]{1,0:T(8,128)}, f32[768,768]{1,0:T(8,128)}, f32[768,768]{1,0:T(8,128)}, f32[768,768]{1,0:T(8,128)}), (f32[768,768]{1,0:T(8,128)}, f32[768,768]{1,0:T(8,128)}, f32[768,768]{1,0:T(8,128)}, ...) | async-done | bytes 9437200 | tf_op jit(solution)/shard_map/psum | solution.py:192
  629.5 3.4 copy.70
  632.9 1.4 copy.71
  635.4 1.4 copy.72
  638.0 1.4 copy.73
  640.5 1.4 copy.74
  643.0 1.4 copy.75
  (164 shorter events, 23.2 us)
Async XLA Ops:
  7.2 182.7 %copy-start = (bf16[768,768]{1,0:T(8,128)(2,1)S(1)}, bf16[768,768]{1,0:T(8,128)(2,1)}, u32[]{:S(2)}) copy-start(bf16[768,768]{1,0:T(8,128)(2,1)} %param.38) | copy-start | bytes 3538948
  7.2 2.0 copy-start.4
  7.2 2.6 copy-start.38
  7.2 2.6 copy-start.53
  7.2 2.6 copy-start.49
  7.2 118.8 %all-gather.3.cloned.1.call-start = ((), (), s32[]{:S(2)}) async-start(), calls=%async_computation.2 | async-start | bytes 3932160 | tf_op jit(solution)/shard_map/all_gather | solution.py:129
  7.3 2.5 copy-start.47
  11.9 3.0 copy-start.50
  24.0 3.1 copy-start.11
  24.0 3.1 copy-start.13
  27.1 2.0 copy-start.31
  27.1 2.0 copy-start.51
  34.1 12.6 %copy-start.7 = (f32[512,768]{0,1:T(8,128)S(1)}, f32[512,768]{0,1:T(8,128)}, u32[]{:S(2)}) copy-start(f32[512,768]{0,1:T(8,128)} %copy.49) | copy-start | bytes 4718596
  46.7 9.7 %copy-start.2 = (f32[12,512,512]{1,2,0:T(8,128)}, f32[12,512,512]{1,2,0:T(8,128)S(1)}, u32[]{:S(2)}) copy-start(f32[12,512,512]{1,2,0:T(8,128)S(1)} %get-tuple-element.69) | copy-start | bytes 37748740
  46.7 9.7 %copy-start.45 = (bf16[768,768]{1,0:T(8,128)(2,1)S(1)}, bf16[768,768]{1,0:T(8,128)(2,1)}, u32[]{:S(2)}) copy-start(bf16[768,768]{1,0:T(8,128)(2,1)} %param.29) | copy-start | bytes 3538948
  46.7 9.7 %copy-start.52 = (f32[768]{0:T(1024)S(1)}, f32[768]{0:T(1024)}, u32[]{:S(2)}) copy-start(f32[768]{0:T(1024)} %param.33) | copy-start | bytes 9220
  59.7 130.1 %all-gather.5.cloned.1.call-start = ((), (), s32[]{:S(2)}) async-start(), calls=%async_computation.4 | async-start | bytes 3932160 | tf_op jit(solution)/shard_map/all_gather | solution.py:142
  60.5 129.4 %copy-start.41 = (f32[768]{0:T(1024)S(1)}, f32[768]{0:T(1024)}, u32[]{:S(2)}) copy-start(f32[768]{0:T(1024)} %param.37) | copy-start | bytes 9220
  60.5 213.8 %reduce-scatter.5.cloned.1.call-start = ((), (), s32[]{:S(2)}) async-start(), calls=%async_computation.5 | async-start | bytes 3932160 | tf_op jit(solution)/shard_map/reduce_scatter | solution.py:148
  189.8 21.3 %copy-start.44 = (bf16[768,768]{1,0:T(8,128)(2,1)S(1)}, bf16[768,768]{1,0:T(8,128)(2,1)}, u32[]{:S(2)}) copy-start(bf16[768,768]{1,0:T(8,128)(2,1)} %param.36) | copy-start | bytes 3538948
  209.4 1.8 copy-start.54
  215.2 121.5 %reduce-scatter.3.cloned.1.call-start = ((), (), s32[]{:S(2)}) async-start(), calls=%async_computation.3 | async-start | bytes 3932160 | tf_op jit(solution)/shard_map/reduce_scatter | solution.py:133
  226.4 244.1 %all-reduce.12.cloned.1.call-start = ((), (), s32[]{:S(2)}) async-start(), calls=%async_computation.7 | async-start | bytes 9437184 | tf_op jit(solution)/shard_map/psum | solution.py:154
  226.5 7.2 %copy-start.25 = (bf16[2048,768]{1,0:T(8,128)(2,1)S(1)}, bf16[2048,768]{1,0:T(8,128)(2,1)}, u32[]{:S(2)}) copy-start(bf16[2048,768]{1,0:T(8,128)(2,1)} %copy-done.24) | copy-start | bytes 9437188
  226.5 7.1 %copy-start.43 = (bf16[2048,768]{1,0:T(8,128)(2,1)S(1)}, bf16[2048,768]{1,0:T(8,128)(2,1)}, u32[]{:S(2)}) copy-start(bf16[2048,768]{1,0:T(8,128)(2,1)} %all-gather.5.cloned.1.call-done) | copy-start | bytes 9437188
  237.8 98.9 %copy-start.42 = (f32[768]{0:T(1024)S(1)}, f32[768]{0:T(1024)}, u32[]{:S(2)}) copy-start(f32[768]{0:T(1024)} %param.39) | copy-start | bytes 9220
  237.8 391.7 %all-reduce.10.cloned.1.call-start = ((), (), s32[]{:S(2)}) async-start(), calls=%async_computation.6 | async-start | bytes 18874368 | tf_op jit(solution)/shard_map/psum | solution.py:192
  276.6 63.6 %copy-start.19 = (bf16[512,768]{1,0:T(8,128)(2,1)S(1)}, bf16[512,768]{1,0:T(8,128)(2,1)}, u32[]{:S(2)}) copy-start(bf16[512,768]{1,0:T(8,128)(2,1)} %param.21) | copy-start | bytes 2359300
  340.2 1.8 copy-start.46
  343.5 10.5 %copy-start.21 = (f32[12,64,512]{2,1,0:T(8,128)S(1)}, f32[12,64,512]{2,1,0:T(8,128)}, u32[]{:S(2)}) copy-start(f32[12,64,512]{2,1,0:T(8,128)} %get-tuple-element.71) | copy-start | bytes 4718596
  364.1 13.0 %copy-start.16 = (f32[512,12,32]{0,2,1:T(8,128)S(1)}, f32[512,12,32]{0,2,1:T(8,128)}, u32[]{:S(2)}) copy-start(f32[512,12,32]{0,2,1:T(8,128)} %copy-done.15) | copy-start | bytes 2359300
  364.1 13.0 %copy-start.18 = (f32[512,12,32]{0,2,1:T(8,128)S(1)}, f32[512,12,32]{0,2,1:T(8,128)}, u32[]{:S(2)}) copy-start(f32[512,12,32]{0,2,1:T(8,128)} %copy-done.17) | copy-start | bytes 2359300
  377.1 1.7 copy-start.12
  380.5 10.1 %slice-start = ((s8[12582912]{0:T(1024)(128)(4,1)}), s8[4194304]{0:T(1024)(128)(4,1)S(1)}, s32[]{:S(2)}) async-start(s8[12582912]{0:T(1024)(128)(4,1)} %bitcast.82), calls=%async_computation.8 | async-start | bytes 8388608
  381.2 1.8 copy-start.23
  381.2 9.4 %slice-start.1 = ((s8[12582912]{0:T(1024)(128)(4,1)}), s8[4194304]{0:T(1024)(128)(4,1)S(1)}, s32[]{:S(2)}) async-start(s8[12582912]{0:T(1024)(128)(4,1)} %bitcast.82), calls=%async_computation.9 | async-start | bytes 8388608
  381.4 3.8 copy-start.33
  383.0 5.1 copy-start.35
  385.1 5.4 slice-start.2
  405.2 15.0 %copy-start.34 = (bf16[512,12,64]{0,2,1:T(8,128)(2,1)S(1)}, bf16[512,12,64]{0,2,1:T(8,128)(2,1)}, u32[]{:S(2)}) copy-start(bf16[512,12,64]{0,2,1:T(8,128)(2,1)} %copy-done.33) | copy-start | bytes 2359300
  420.2 2.3 copy-start.36
  420.2 2.3 copy-start.48
  629.5 3.4 copy-start.30
  632.9 2.5 copy-start.29
  635.4 2.5 copy-start.28
  638.0 2.5 copy-start.27
  640.5 2.5 copy-start.26
  640.5 3.9 copy-start.1
  (16 other events, 20.3 us)
Sparse Core Ops, SparseCore 0:
  59.9 66.1 all-gather.2
  127.7 62.1 all-gather.4
  215.4 58.8 reduce-scatter.4
  276.4 60.2 reduce-scatter.2
  340.5 87.1 all-reduce.11
  436.6 192.8 all-reduce.9
where the time goes:
time: 661 us; the launch traced here: 651 us
  waiting for transfers between devices  378 us (57%)
  matrix products  144 us (22%)
  blocking collectives  57 us (9%)
  local copies, waits for them, and re-layouts  34.7 us (5%)
  other arithmetic  22.8 us (3%)
  between operations  15 us (2%)
    psum x1, waiting for transfers between devices, body(): lax.psum((gain_one_grad, bias_one_grad, query_weight_grad, wkey_grad, val...  159 us
    all_gather x1, waiting for transfers between devices, body(): gathered = lax.all_gather(second_low, 'tensor', axis=0, tiled=True)  65.5 us
    reduce_scatter x1, waiting for transfers between devices, body(): lax.psum_scatter(matmul(lax.slice_in_dim(hidden_low, 0, row_count * lax.a...  60.1 us
    all_gather x1, waiting for transfers between devices, body(): cot_gathered = lax.all_gather(cotangent, 'tensor', axis=0, tiled=True)  56.3 us
    psum x1, blocking collectives, body(): lax.psum((gain_one_grad, bias_one_grad, query_weight_grad, wkey_grad, val...  42.2 us
    reduce_scatter x1, waiting for transfers between devices, body(): lax.psum_scatter(right_product(inner_grad, w_up).astype(jnp.bfloat16), 't...  36 us
    dot_general x3, matrix products, attend(): jnp.einsum('otg,atg->toa', query_feature_map, key_feature_map, precision=...  34.1 us
    dot_general x3, matrix products, attend(): jnp.einsum('hqk,khd->qhd', weights, value_heads, precision=highest_precis...  32.3 us
  transfers between devices with their start and end apart: 6, of which 5 were waited for; matrix products, arithmetic and copies ran while one was open for 16% of the time, Pallas kernels for 0%

commit v1 on v0

--- a/solution.py
+++ b/solution.py
@@ -4,6 +4,7 @@
 import jax.numpy as jnp
 from jax import lax
 from jax.sharding import PartitionSpec as P
+from jax.lax import axis_index, axis_size, ppermute
 
 HEADS = 12
 highest_precision = lax.Precision.HIGHEST
@@ -139,7 +140,30 @@
         tiled=True,
     ).astype(jnp.float32)
     output = (middle + branch + b_down).astype(jnp.bfloat16)
-    cot_gathered = lax.all_gather(cotangent, "tensor", axis=0, tiled=True)
+    v_next, big, z = (axis_size("tensor"), axis_index("tensor"), cotangent.shape[0])
+    cot_gathered = lax.dynamic_update_slice_in_dim(
+        jnp.zeros(
+            [u * v_next if s == 0 else u for s, u in enumerate(cotangent.shape)], cotangent.dtype
+        ),
+        cotangent,
+        big * z,
+        axis=0,
+    )
+    finding = b_now = cotangent
+    for j in range(1, v_next // 2 + 1):
+        finding = ppermute(
+            finding, axis_name="tensor", perm=[(s, (s + 1) % v_next) for s in range(v_next)]
+        )
+        cot_gathered = lax.dynamic_update_slice_in_dim(
+            cot_gathered, finding, (big - j) % v_next * z, axis=0
+        )
+        if 2 * j < v_next:
+            b_now = ppermute(
+                b_now, axis_name="tensor", perm=[(s, (s - 1) % v_next) for s in range(v_next)]
+            )
+            cot_gathered = lax.dynamic_update_slice_in_dim(
+                cot_gathered, b_now, (big + j) % v_next * z, axis=0
+            )
     down_grad = left_product(hidden_low, cot_gathered)
     hidden_grad = right_product(cot_gathered, w_down)
     inner_grad = gelu_back(hidden_grad)[0].astype(jnp.bfloat16)

time: 661 us -> 646 us (0.977)
  waiting for transfers between devices: 378 us -> 329 us
  starting transfers between devices: 0.65 us -> 27.9 us
  local copies, waits for them, and re-layouts: 34.7 us -> 43.8 us
    ppermute x0 -> x3, waiting for transfers between devices: none -> 64.3 us  [the longest x2 43.2 us: body(): ppermute(finding, axis_name='tensor', perm=[(s, (s + 1) % v_next) for s i...]
    all_gather x1, waiting for transfers between devices: 65.5 us -> 6.69 us  [body(): gathered = lax.all_gather(second_low, 'tensor', axis=0, tiled=True)]
    all_gather x1 -> x0, waiting for transfers between devices: 56.3 us -> none  [body(): cot_gathered = lax.all_gather(cotangent, 'tensor', axis=0, tiled=True)]
    ppermute x0 -> x3, starting transfers between devices: none -> 27.3 us  [the longest x2 25.2 us: body(): ppermute(finding, axis_name='tensor', perm=[(s, (s + 1) % v_next) for s i...]
    dynamic_update_slice x0 -> x4, local copies, waits for them, and re-layouts: none -> 7.24 us  [the longest x2 4.18 us: body(): lax.dynamic_update_slice_in_dim(cot_gathered, finding, (big - j) % v_next...]
    unnamed x122 -> x126, local copies, waits for them, and re-layouts: 25.4 us -> 25.3 us
  transfers between devices with their start and end apart: 6 -> 8, of which waited for: 5 -> 7; matrix products, arithmetic and copies ran while one was open for 16% -> 16% of each run, Pallas kernels for 0% -> 0%
where the time goes in v1:
time: 646 us; the launch traced here: 636 us
  waiting for transfers between devices  329 us (51%)
  matrix products  141 us (22%)
  blocking collectives  57 us (9%)
  local copies, waits for them, and re-layouts  43.8 us (7%)
  starting transfers between devices  27.9 us (4%)
  other arithmetic  22.7 us (4%)
  between operations  15 us (2%)
    psum x1, waiting for transfers between devices, body(): lax.psum((gain_one_grad, bias_one_grad, query_weight_grad, wkey_grad, val...  159 us
    reduce_scatter x1, waiting for transfers between devices, body(): lax.psum_scatter(matmul(lax.slice_in_dim(hidden_low, 0, row_count * lax.a...  60.3 us
    ppermute x2, waiting for transfers between devices, body(): ppermute(finding, axis_name='tensor', perm=[(s, (s + 1) % v_next) for s i...  43.2 us
    psum x1, blocking collectives, body(): lax.psum((gain_one_grad, bias_one_grad, query_weight_grad, wkey_grad, val...  42.2 us
    reduce_scatter x1, waiting for transfers between devices, body(): lax.psum_scatter(right_product(inner_grad, w_up).astype(jnp.bfloat16), 't...  38.7 us
    dot_general x3, matrix products, attend(): jnp.einsum('otg,atg->toa', query_feature_map, key_feature_map, precision=...  33.8 us
    dot_general x3, matrix products, attend(): jnp.einsum('hqk,khd->qhd', weights, value_heads, precision=highest_precis...  32.8 us
    dot_general x6, matrix products, right_product(): lax.dot_general(left, right, (((1,), (1,)), ((), ())), preferred_element_...  28.8 us
  transfers between devices with their start and end apart: 8, of which 7 were waited for; matrix products, arithmetic and copies ran while one was open for 16% of the time, Pallas kernels for 0%

profile of v1, /device:TPU:0, one launch (start us, length us, event | category | flops | bytes accessed | tf_op | source)
XLA Modules:
  0.0 636.5 jit_solution(9299695469706524760)
XLA Ops:
  9.8 2.1 convolution_add_fusion.1
  11.9 3.0 copy.50
  14.9 3.3 convolution_add_fusion
  18.3 3.0 copy.51
  21.6 2.3 multiply_subtract_fusion.1
  25.1 2.0 fusion.53
  27.1 2.0 fusion.59
  29.0 2.1 convolution_add_fusion.2
  31.1 3.0 copy.49
  34.1 12.3 %multiply_reduce_fusion = (f32[12,512]{1,0:T(8,128)S(1)}, f32[12,512,512]{1,2,0:T(8,128)S(1)}) fusion(f32[512,512]{0,1:T(8,128)S(1)} %compare_convert_fusion, f32[512,12,32]{0,2,1:T(8,128)} %fusion.59, f32[512,12,32]{0,2,1:T(8,128)} %fusion.53), kind=kOutput, calls=%fused_computation.5 | convolution fusion | flops 1214638080 | bytes 15228928 | tf_op jit(solution)/shard_map/jvp(otg,atg->toa)/dot_general | solution.py:59
  46.5 9.9 %fusion.37 = (bf16[512,12,64]{0,2,1:T(8,128)(2,1)S(1)}, f32[12,64,512]{2,1,0:T(8,128)}) fusion(f32[512,12]{0,1:T(8,128)S(1)} %bitcast.95, f32[512,12,64]{0,2,1:T(8,128)S(1)} %bitcast.84, f32[12,512,512]{1,2,0:T(8,128)S(1)} %get-tuple-element.69, f32[512,512]{0,1:T(8,128)S(1)} %compare_convert_fusion), kind=kOutput, calls=%fused_computation.67 | convolution fusion | flops 2419851264 | bytes 17588224 | tf_op jit(solution)/shard_map/jvp(hqk,khd->qhd)/dot_general | solution.py:65
  59.8 3.1 collective-permute-start
  62.8 2.1 collective-permute-start.1
  64.9 26.9 %collective-permute-done = bf16[512,768]{1,0:T(8,128)(2,1)} collective-permute-done((bf16[512,768]{1,0:T(8,128)(2,1)}, bf16[512,768]{1,0:T(8,128)(2,1)}, u32[]{:S(2)}, u32[]{:S(2)}) %collective-permute-start) | collective-permute-done | bytes 786464 | tf_op jit(solution)/shard_map/ppermute | solution.py:154
  91.9 22.1 %collective-permute-start.2 = (bf16[512,768]{1,0:T(8,128)(2,1)}, bf16[512,768]{1,0:T(8,128)(2,1)}, u32[]{:S(2)}, u32[]{:S(2)}) collective-permute-start(bf16[512,768]{1,0:T(8,128)(2,1)} %collective-permute-done), channel_id=1, source_target_pairs={{0,1},{1,2},{2,3},{3,0},{4,5},{5,6},{6,7},{7,4},{8,9},{9,10},{10,1... | collective-permute-start | bytes 2359304 | tf_op jit(solution)/shard_map/ppermute | solution.py:154
  114.0 2.0 broadcast_in_dim.14
  117.0 2.1 constant_dynamic-update-slice_fusion.2
  119.1 21.1 %collective-permute-done.1 = bf16[512,768]{1,0:T(8,128)(2,1)} collective-permute-done((bf16[512,768]{1,0:T(8,128)(2,1)}, bf16[512,768]{1,0:T(8,128)(2,1)}, u32[]{:S(2)}, u32[]{:S(2)}) %collective-permute-start.1) | collective-permute-done | bytes 786464 | tf_op jit(solution)/shard_map/ppermute | solution.py:161
  140.1 2.1 constant_dynamic-update-slice_fusion.1
  142.2 16.3 %collective-permute-done.2 = bf16[512,768]{1,0:T(8,128)(2,1)} collective-permute-done((bf16[512,768]{1,0:T(8,128)(2,1)}, bf16[512,768]{1,0:T(8,128)(2,1)}, u32[]{:S(2)}, u32[]{:S(2)}) %collective-permute-start.2) | collective-permute-done | bytes 786464 | tf_op jit(solution)/shard_map/ppermute | solution.py:154
  158.5 2.1 constant_dynamic-update-slice_fusion
  160.6 6.7 %all-gather.2.cloned.1.call-done = bf16[2048,768]{1,0:T(8,128)(2,1)} async-done(((bf16[512,768]{1,0:T(8,128)(2,1)}), bf16[2048,768]{1,0:T(8,128)(2,1)}) %all-gather.2.cloned.1.call-update) | async-done | bytes 3145744 | tf_op jit(solution)/shard_map/all_gather | solution.py:130
  167.3 4.9 fusion.109
  172.2 19.7 %convert_reduce_fusion = (f32[768]{0:T(1024)S(1)}, bf16[2048,768]{1,0:T(8,128)(2,1)S(1)}, f32[2048,768]{1,0:T(8,128)}) fusion(f32[2048,768]{1,0:T(8,128)S(1)} %fusion.109, f32[768]{0:T(1024)S(1)} %copy-done.42, bf16[2048,768]{1,0:T(8,128)(2,1)} %constant_dynamic-update-slice_fusion, bf16[768,768]{1,0:T(8,128)(2,1)S(1)} %copy-done), kind=kOutput, calls=%fused_computation.10 | convolution fusion | flops 2533883136 | bytes 20060160 | tf_op jit(solution)/shard_map/dot_general | solution.py:80
  193.5 4.0 convolution_convert_fusion
  197.8 5.5 multiply_convert_fusion
  204.9 4.0 convolution_convert_fusion.1
  209.0 7.1 %fusion.115 = f32[768,768]{1,0:T(8,128)} fusion(bf16[2048,768]{1,0:T(8,128)(2,1)} %copy-done.26, bf16[2048,768]{1,0:T(8,128)(2,1)} %constant_dynamic-update-slice_fusion), kind=kOutput, calls=%fused_computation.177 | convolution fusion | flops 2415919104 | bytes 8650752 | tf_op jit(solution)/shard_map/dot_general | solution.py:74
  216.1 4.2 fusion.114
  220.5 38.7 %reduce-scatter.5.cloned.1.call-done = bf16[512,768]{1,0:T(8,128)(2,1)} async-done(((bf16[2048,768]{1,0:T(8,128)(2,1)}), bf16[512,768]{1,0:T(8,128)(2,1)}) %reduce-scatter.5.cloned.1.call-update) | async-done | bytes 786448 | tf_op jit(solution)/shard_map/reduce_scatter | solution.py:172
  259.2 2.3 fusion.33
  261.5 60.3 %reduce-scatter.3.cloned.1.call-done = bf16[512,768]{1,0:T(8,128)(2,1)} async-done(((bf16[2048,768]{1,0:T(8,128)(2,1)}), bf16[512,768]{1,0:T(8,128)(2,1)}) %reduce-scatter.3.cloned.1.call-update) | async-done | bytes 786448 | tf_op jit(solution)/shard_map/reduce_scatter | solution.py:134
  321.8 3.5 fusion.105
  328.6 10.7 %fusion.35 = f32[12,512,512]{1,2,0:T(8,128)S(1)} fusion(f32[512,12,64]{0,2,1:T(8,128)S(1)} %bitcast.85, f32[512,12,64]{0,2,1:T(8,128)S(1)} %bitcast.86, f32[512,12]{0,1:T(8,128)S(1)} %bitcast.96), kind=kOutput, calls=%fused_computation.63 | convolution fusion | flops 2416312320 | bytes 15753216 | tf_op jit(solution)/shard_map/transpose(jvp(hqk,khd->qhd))/dot_general | solution.py:65
  340.8 8.6 %fusion.108 = (f32[512,12]{0,1:T(8,128)S(1)}, f32[512,12,32]{0,2,1:T(8,128)S(1)}) fusion(f32[512,12,32]{0,2,1:T(8,128)S(1)} %copy-done.9, f32[512,12,32]{0,2,1:T(8,128)S(1)} %copy-done.10, f32[12,512,512]{1,2,0:T(8,128)S(1)} %fusion.35, f32[12,512]{1,0:T(8,128)S(1)} %negate_bitcast_fusion, f32[512,512]{0,1:T(8,128)S(1)} %compare_convert_fusion), kind=kOutput, calls=%fused_computation.170 | convolution fusion | flops 1215031296 | bytes 16039936 | tf_op jit(solution)/shard_map/transpose(jvp(otg,atg->toa))/dot_general | solution.py:59
  349.4 12.9 %fusion.107 = (f32[512,12]{0,1:T(8,128)S(1)}, f32[512,12,32]{0,2,1:T(8,128)S(1)}) fusion(f32[512,12,32]{0,2,1:T(8,128)S(1)} %copy-done.10, f32[512,12,32]{0,2,1:T(8,128)S(1)} %copy-done.9, f32[12,512,512]{1,2,0:T(8,128)S(1)} %fusion.35, f32[12,512]{1,0:T(8,128)S(1)} %negate_bitcast_fusion, f32[512,512]{0,1:T(8,128)S(1)} %compare_convert_fusion), kind=kOutput, calls=%fused_computation.169 | convolution fusion | flops 1215031296 | bytes 16039936 | tf_op jit(solution)/shard_map/transpose(jvp(otg,atg->toa))/dot_general | solution.py:59
  362.4 1.7 fusion.40
  364.1 1.7 fusion.39
  368.3 2.2 fusion.113
  370.4 2.7 fusion.95
  373.2 2.5 fusion.97
  375.7 12.1 %convert_reduce_fusion.5 = (f32[12,64]{1,0:T(8,128)S(1)}, bf16[12,64,512]{2,1,0:T(8,128)(2,1)S(1)}) fusion(f32[12,512,512]{1,2,0:T(8,128)S(1)} %bitcast.83, f32[512,512]{0,1:T(8,128)S(1)} %compare_convert_fusion, f32[512,12,64]{0,2,1:T(8,128)S(1)} %bitcast.88, f32[512,12]{0,1:T(8,128)S(1)} %bitcast.97), kind=kOutput, calls=%fused_computation.74 | convolution fusion | flops 2420636928 | bytes 16018432 | tf_op jit(solution)/shard_map/transpose(jvp(hqk,khd->qhd))/dot_general | solution.py:65
  387.8 2.5 fusion.93
  390.3 14.8 %psum.125 = f32[768]{0:T(1024)} all-reduce(f32[768]{0:T(1024)S(1)} %get-tuple-element.40), channel_id=1, replica_groups=mesh['dp'=8,'tensor'=4] {'dp'}, use_global_device_ids=true, to_apply=%region_39.40 | all-reduce | flops 768 | bytes 6144 | tf_op jit(solution)/shard_map/psum | solution.py:178
  405.4 2.3 fusion.112
  413.5 42.2 %all-reduce.4 = (f32[768]{0:T(1024)}, f32[768]{0:T(1024)}, f32[768]{0:T(1024)}, f32[768]{0:T(1024)}, f32[768]{0:T(1024)}, /*index=5*/f32[768]{0:T(1024)}, f32[768]{0:T(1024)}, f32[768]{0:T(1024)}, f32[768]{0:T(1024)}) all-reduce(f32[768]{0:T(1024)S(1)} %get-tuple-element.18, ...), channel_id=1, replica_groups=mesh['dp'=8,'tensor'=4] {'dp','tensor'}, use_global_device_ids=true, to_apply=%region_18.19 | all-reduce | flops 6912 | bytes 55296 | tf_op jit(solution)/shard_map/psum | solution.py:216
  455.6 159.0 %all-reduce.10.cloned.1.call-done = (f32[768,768]{1,0:T(8,128)}, f32[768,768]{1,0:T(8,128)}, f32[768,768]{1,0:T(8,128)}, f32[768,768]{1,0:T(8,128)}) async-done(((f32[768,768]{1,0:T(8,128)}, f32[768,768]{1,0:T(8,128)}, f32[768,768]{1,0:T(8,128)}, f32[768,768]{1,0:T(8,128)}), (f32[768,768]{1,0:T(8,128)}, f32[768,768]{1,0:T(8,128)}, f32[768,768]{1,0:T(8,128)}, ...) | async-done | bytes 9437200 | tf_op jit(solution)/shard_map/psum | solution.py:216
  614.6 3.4 copy.74
  (176 shorter events, 36.7 us)
Async XLA Ops:
  7.2 165.0 %copy-start = (bf16[768,768]{1,0:T(8,128)(2,1)S(1)}, bf16[768,768]{1,0:T(8,128)(2,1)}, u32[]{:S(2)}) copy-start(bf16[768,768]{1,0:T(8,128)(2,1)} %param.38) | copy-start | bytes 3538948
  7.2 2.0 copy-start.4
  7.2 2.6 copy-start.39
  7.2 2.6 copy-start.54
  7.2 2.6 copy-start.50
  7.2 160.0 %all-gather.2.cloned.1.call-start = ((), (), s32[]{:S(2)}) async-start(), calls=%async_computation.2 | async-start | bytes 3932160 | tf_op jit(solution)/shard_map/all_gather | solution.py:130
  7.3 2.5 copy-start.48
  11.9 3.0 copy-start.51
  24.0 3.1 copy-start.11
  24.0 3.1 copy-start.13
  27.1 2.0 copy-start.32
  27.1 2.0 copy-start.52
  34.1 12.3 %copy-start.7 = (f32[512,768]{0,1:T(8,128)S(1)}, f32[512,768]{0,1:T(8,128)}, u32[]{:S(2)}) copy-start(f32[512,768]{0,1:T(8,128)} %copy.49) | copy-start | bytes 4718596
  46.4 9.9 %copy-start.2 = (f32[12,512,512]{1,2,0:T(8,128)}, f32[12,512,512]{1,2,0:T(8,128)S(1)}, u32[]{:S(2)}) copy-start(f32[12,512,512]{1,2,0:T(8,128)S(1)} %get-tuple-element.69) | copy-start | bytes 37748740
  46.5 9.9 %copy-start.46 = (bf16[768,768]{1,0:T(8,128)(2,1)S(1)}, bf16[768,768]{1,0:T(8,128)(2,1)}, u32[]{:S(2)}) copy-start(bf16[768,768]{1,0:T(8,128)(2,1)} %param.29) | copy-start | bytes 3538948
  46.5 9.9 %copy-start.53 = (f32[768]{0:T(1024)S(1)}, f32[768]{0:T(1024)}, u32[]{:S(2)}) copy-start(f32[768]{0:T(1024)} %param.33) | copy-start | bytes 9220
  59.7 199.5 %reduce-scatter.5.cloned.1.call-start = ((), (), s32[]{:S(2)}) async-start(), calls=%async_computation.4 | async-start | bytes 3932160 | tf_op jit(solution)/shard_map/reduce_scatter | solution.py:172
  59.8 32.1 %collective-permute-start = (bf16[512,768]{1,0:T(8,128)(2,1)}, bf16[512,768]{1,0:T(8,128)(2,1)}, u32[]{:S(2)}, u32[]{:S(2)}) collective-permute-start(bf16[512,768]{1,0:T(8,128)(2,1)} %param.21), channel_id=1, source_target_pairs={{0,1},{1,2},{2,3},{3,0},{4,5},{5,6},{6,7},{7,4},{8,9},{9,10},{10,1... | collective-permute-start | bytes 2359304 | tf_op jit(solution)/shard_map/ppermute | solution.py:154
  62.8 77.3 %collective-permute-start.1 = (bf16[512,768]{1,0:T(8,128)(2,1)}, bf16[512,768]{1,0:T(8,128)(2,1)}, u32[]{:S(2)}, u32[]{:S(2)}) collective-permute-start(bf16[512,768]{1,0:T(8,128)(2,1)} %param.21), channel_id=1, source_target_pairs={{0,3},{1,0},{2,1},{3,2},{4,7},{5,4},{6,5},{7,6},{8,11},{9,8},{10,9... | collective-permute-start | bytes 2359304 | tf_op jit(solution)/shard_map/ppermute | solution.py:161
  91.9 66.6 %collective-permute-start.2 = (bf16[512,768]{1,0:T(8,128)(2,1)}, bf16[512,768]{1,0:T(8,128)(2,1)}, u32[]{:S(2)}, u32[]{:S(2)}) collective-permute-start(bf16[512,768]{1,0:T(8,128)(2,1)} %collective-permute-done), channel_id=1, source_target_pairs={{0,1},{1,2},{2,3},{3,0},{4,5},{5,6},{6,7},{7,4},{8,9},{9,10},{10,1... | collective-permute-start | bytes 2359304 | tf_op jit(solution)/shard_map/ppermute | solution.py:154
  114.0 2.0 copy-start.19
  160.6 11.6 %copy-start.42 = (f32[768]{0:T(1024)S(1)}, f32[768]{0:T(1024)}, u32[]{:S(2)}) copy-start(f32[768]{0:T(1024)} %param.37) | copy-start | bytes 9220
  172.2 19.7 %copy-start.22 = (f32[2048,768]{1,0:T(8,128)}, f32[2048,768]{1,0:T(8,128)S(1)}, u32[]{:S(2)}) copy-start(f32[2048,768]{1,0:T(8,128)S(1)} %fusion.109) | copy-start | bytes 18874372
  172.2 21.3 %copy-start.45 = (bf16[768,768]{1,0:T(8,128)(2,1)S(1)}, bf16[768,768]{1,0:T(8,128)(2,1)}, u32[]{:S(2)}) copy-start(bf16[768,768]{1,0:T(8,128)(2,1)} %param.36) | copy-start | bytes 3538948
  197.6 124.3 %reduce-scatter.3.cloned.1.call-start = ((), (), s32[]{:S(2)}) async-start(), calls=%async_computation.3 | async-start | bytes 3932160 | tf_op jit(solution)/shard_map/reduce_scatter | solution.py:134
  208.9 246.7 %all-reduce.12.cloned.1.call-start = ((), (), s32[]{:S(2)}) async-start(), calls=%async_computation.6 | async-start | bytes 9437184 | tf_op jit(solution)/shard_map/psum | solution.py:178
  209.0 7.1 %copy-start.44 = (bf16[2048,768]{1,0:T(8,128)(2,1)S(1)}, bf16[2048,768]{1,0:T(8,128)(2,1)}, u32[]{:S(2)}) copy-start(bf16[2048,768]{1,0:T(8,128)(2,1)} %all-gather.2.cloned.1.call-done) | copy-start | bytes 9437188
  209.0 7.1 %copy-start.56 = (bf16[2048,768]{1,0:T(8,128)(2,1)S(1)}, bf16[2048,768]{1,0:T(8,128)(2,1)}, u32[]{:S(2)}) copy-start(bf16[2048,768]{1,0:T(8,128)(2,1)} %copy-done.55) | copy-start | bytes 9437188
  220.3 101.6 %copy-start.43 = (f32[768]{0:T(1024)S(1)}, f32[768]{0:T(1024)}, u32[]{:S(2)}) copy-start(f32[768]{0:T(1024)} %param.39) | copy-start | bytes 9220
  220.3 394.4 %all-reduce.10.cloned.1.call-start = ((), (), s32[]{:S(2)}) async-start(), calls=%async_computation.5 | async-start | bytes 18874368 | tf_op jit(solution)/shard_map/psum | solution.py:216
  261.5 63.8 %copy-start.20 = (bf16[512,768]{1,0:T(8,128)(2,1)S(1)}, bf16[512,768]{1,0:T(8,128)(2,1)}, u32[]{:S(2)}) copy-start(bf16[512,768]{1,0:T(8,128)(2,1)} %param.21) | copy-start | bytes 2359300
  328.6 10.7 %copy-start.23 = (f32[12,64,512]{2,1,0:T(8,128)S(1)}, f32[12,64,512]{2,1,0:T(8,128)}, u32[]{:S(2)}) copy-start(f32[12,64,512]{2,1,0:T(8,128)} %get-tuple-element.71) | copy-start | bytes 4718596
  349.4 12.9 %copy-start.16 = (f32[512,12,32]{0,2,1:T(8,128)S(1)}, f32[512,12,32]{0,2,1:T(8,128)}, u32[]{:S(2)}) copy-start(f32[512,12,32]{0,2,1:T(8,128)} %copy-done.15) | copy-start | bytes 2359300
  349.4 12.9 %copy-start.18 = (f32[512,12,32]{0,2,1:T(8,128)S(1)}, f32[512,12,32]{0,2,1:T(8,128)}, u32[]{:S(2)}) copy-start(f32[512,12,32]{0,2,1:T(8,128)} %copy-done.17) | copy-start | bytes 2359300
  365.8 9.9 %slice-start = ((s8[12582912]{0:T(1024)(128)(4,1)}), s8[4194304]{0:T(1024)(128)(4,1)S(1)}, s32[]{:S(2)}) async-start(s8[12582912]{0:T(1024)(128)(4,1)} %bitcast.82), calls=%async_computation.7 | async-start | bytes 8388608
  366.5 9.2 %slice-start.1 = ((s8[12582912]{0:T(1024)(128)(4,1)}), s8[4194304]{0:T(1024)(128)(4,1)S(1)}, s32[]{:S(2)}) async-start(s8[12582912]{0:T(1024)(128)(4,1)} %bitcast.82), calls=%async_computation.8 | async-start | bytes 8388608
  366.7 3.8 copy-start.34
  368.2 4.9 copy-start.36
  370.4 5.2 slice-start.2
  390.3 15.1 %copy-start.35 = (bf16[512,12,64]{0,2,1:T(8,128)(2,1)S(1)}, bf16[512,12,64]{0,2,1:T(8,128)(2,1)}, u32[]{:S(2)}) copy-start(bf16[512,12,64]{0,2,1:T(8,128)(2,1)} %copy-done.34) | copy-start | bytes 2359300
  405.4 2.3 copy-start.37
  405.4 2.3 copy-start.49
  614.6 3.4 copy-start.31
  618.0 2.5 copy-start.30
  620.5 2.5 copy-start.29
  623.0 2.5 copy-start.28
  625.6 2.5 copy-start.27
  625.6 3.9 copy-start.1
  (20 other events, 27.2 us)
Sparse Core Ops, SparseCore 0:
  59.8 107.3 all-gather.1
  197.7 61.4 reduce-scatter.4
  261.5 60.2 reduce-scatter.2
  325.6 87.1 all-reduce.11
  421.7 192.8 all-reduce.9
